TPU v7x, 32 devices: a whole 2x2x4 slice. The times are simulated.
32 devices in a mesh: row: 4 (over y, core), col: 8 (over z, x).
Axes of the slice: x: 2, y: 2, z: 4, core: 2. Of those that a mesh axis runs over, the one named last changes fastest.
Arguments:
- transition: bfloat16 [32768, 32768], P('row', 'col'), may hold values from 1.5258789e-06 to 0.0024414062, as said below
- emission: bfloat16 [96, 32768], P(None, 'col'), may hold values from 0.0099487305 to 1
- token_ids: int32 [2, 192], replicated, may hold values from 0 to 95
- forward: bfloat16 [2, 192, 32768], P(None, 'col', 'row'), may hold values from 3.0517578e-06 to 0.0008239746, as said below
- backward_last: float32 [192, 32768], P('row', 'col'), may hold values from 0.1 to 10
Outputs:
- backward: float32 [2, 192, 32768], P(None, 'col', 'row')
- counts: float32 [32768, 1024], P('row', 'col')
Inputs may be any that keep to these rules, and one draw needn't show every extreme that they name: Positive transition weights. Positive forward weights.
All inputs are finite; a program needn't handle non-finite values.
Results may differ from a plain program's by a relative error of at most 0.00048.
Values may be sent and summed in bfloat16 or wider, within the bound.
A program may use at most 192 MiB of HBM per device.

v0:
```python
import jax
import jax.numpy as jnp
from jax import lax
from jax.sharding import PartitionSpec as P

H = 32768
N = 192
DW = 128
CHUNKS = 2


def reduce_scatter(partial, scale, col_count, col_index, local_seqs):
    half = col_count // 2
    width = partial.shape[1]
    scaled = (partial * scale).reshape(half, 2, local_seqs, width)
    side = col_index % 2
    away = lax.dynamic_index_in_dim(scaled, 1 - side, 1, keepdims=False).astype(jnp.float16)
    got = lax.ppermute(away, "col", [(c, c ^ 1) for c in range(col_count)])
    pair = lax.dynamic_index_in_dim(scaled, side, 1, keepdims=False) + got.astype(jnp.float32)
    here = col_index // 2
    total = lax.dynamic_index_in_dim(pair, here, 0, keepdims=False)
    packed = pair.astype(jnp.float16)
    for k in range(1, half):
        piece = lax.dynamic_index_in_dim(packed, (here + k) % half, 0, keepdims=False)
        got = lax.ppermute(piece, "col", [(c, (c + 2 * k) % col_count) for c in range(col_count)])
        total = total + got.astype(jnp.float32)
    return total


def on_device(transition, emission, token_ids, forward, backward_last):
    row_count = lax.axis_size("row")
    col_count = lax.axis_size("col")
    row_index = lax.axis_index("row")
    col_index = lax.axis_index("col")
    ratio = col_count // row_count
    local_seqs = forward.shape[1]
    row_seqs = backward_last.shape[0]
    block_src = transition.shape[0]
    block_dst = transition.shape[1]
    seq_total = local_seqs * col_count
    forward_all = [None, lax.all_gather(forward[1], "col", axis=0, tiled=True)]
    columns = lax.broadcasted_iota(jnp.int32, (row_seqs, emission.shape[0]), 1)
    window = transition[:, :DW]
    totals = jnp.zeros((block_src, DW), jnp.float32)
    outputs = [None, None]
    beta = backward_last
    scale = jnp.full((seq_total, 1), 64.0, jnp.float32)
    chunk = block_src // CHUNKS
    for step in (1, 0):
        tokens = lax.dynamic_slice_in_dim(token_ids[step], row_index * row_seqs, row_seqs, 0)
        onehot = (tokens[:, None] == columns).astype(jnp.bfloat16)
        emitted = jnp.dot(onehot, emission, preferred_element_type=jnp.float32)
        local_back = (emitted * beta).astype(jnp.bfloat16)
        weighted_back = lax.all_gather(local_back, "row", axis=0, tiled=True)
        pieces = []
        norm = jnp.zeros((seq_total,), jnp.float32)
        mass = jnp.zeros((seq_total,), jnp.float32)
        if step == 0:
            forward_all[0] = lax.all_gather(forward[0], "col", axis=0, tiled=True)
        for k in range(CHUNKS):
            rows = slice(k * chunk, (k + 1) * chunk)
            partial = lax.dot_general(
                weighted_back,
                transition[rows],
                (((1,), (1,)), ((), ())),
                preferred_element_type=jnp.float32,
            )
            norm = norm + jnp.sum(forward_all[step][:, rows].astype(jnp.float32) * partial, axis=1)
            mass = mass + jnp.sum(partial, axis=1)
            pieces.append(reduce_scatter(partial, scale, col_count, col_index, local_seqs))
        if step == 1:
            both = lax.psum(jnp.stack([norm, mass]), ("row", "col"))
            normal_all = both[0]
        else:
            normal_all = lax.psum(norm, ("row", "col"))
        normal_mine = lax.dynamic_slice_in_dim(normal_all, col_index * local_seqs, local_seqs, 0)
        scale_mine = lax.dynamic_slice_in_dim(scale, col_index * local_seqs, local_seqs, 0)
        mine = jnp.concatenate(pieces, axis=1) / (scale_mine * normal_mine[:, None])
        outputs[step] = mine
        if step == 1:
            halves = mine.reshape(local_seqs, ratio, block_dst)
            arrived = []
            for p in range(ratio):
                part = lax.dynamic_index_in_dim(halves, (col_index + p) % ratio, 1, keepdims=False)
                moves = []
                for r in range(row_count):
                    for c in range(col_count):
                        h = (c + p) % ratio
                        moves.append((r * col_count + c, c // ratio * col_count + r * ratio + h))
                arrived.append(lax.ppermute(part, ("row", "col"), moves))
            turned = jnp.stack([arrived[-i % ratio] for i in range(ratio)] * 2)
            start = (ratio - col_index % ratio) % ratio
            beta = lax.dynamic_slice_in_dim(turned, start, ratio, 0).reshape(row_seqs, block_dst)
            scale = (16777216.0 * both[0] / both[1])[:, None]
        scaled = (forward_all[step].astype(jnp.float32) / normal_all[:, None]).astype(jnp.bfloat16)
        totals = totals + lax.dot_general(
            scaled,
            weighted_back[:, :DW],
            (((0,), (0,)), ((), ())),
            preferred_element_type=jnp.float32,
        )
    counts = window.astype(jnp.float32) * totals * (H * H / N)
    return (jnp.stack(outputs), counts)


def solution(mesh):
    in_specs = (P("row", "col"), P(None, "col"), P(), P(None, "col", "row"), P("row", "col"))
    out_specs = (P(None, "col", "row"), P("row", "col"))
    return jax.shard_map(
        on_device, mesh=mesh, in_specs=in_specs, out_specs=out_specs, check_vma=False
    )
```

profile of v0, /device:TPU:0, one launch (start us, length us, event | category | flops | bytes accessed | tf_op | source)
XLA Modules:
  0.0 469.5 jit_solution(5049262565942433598)
XLA Ops:
  8.3 2.2 fusion.10
  10.6 2.0 fusion.50
  12.8 20.2 %all-gather.7.cloned.1.call-done = bf16[192,4096]{1,0:T(8,128)(2,1)} async-done(((bf16[48,4096]{1,0:T(8,128)(2,1)}), bf16[192,4096]{1,0:T(8,128)(2,1)}) %all-gather.7.cloned.1.call-update) | async-done | bytes 1572880 | tf_op jit(solution)/shard_map/all_gather | solution.py:54
  33.1 21.2 %fusion.6 = f32[192,4096]{1,0:T(8,128)} fusion(bf16[192,4096]{1,0:T(8,128)(2,1)} %all-gather.7.cloned.1.call-done, bf16[8192,4096]{1,0:T(8,128)(2,1)} %param.5), kind=kOutput, calls=%fused_computation.6 | convolution fusion | flops 6442450944 | bytes 38273024 | tf_op jit(solution)/shard_map/dot_general | solution.py:62
  54.3 42.0 %all-gather.11.cloned.1.call-done = bf16[1,192,8192]{2,1,0:T(8,128)(2,1)} async-done(((bf16[1,24,8192]{2,1,0:T(8,128)(2,1)}), bf16[1,192,8192]{2,1,0:T(8,128)(2,1)}) %all-gather.11.cloned.1.call-update) | async-done | bytes 3145744 | tf_op jit(solution)/shard_map/all_gather | solution.py:41
  96.3 20.1 %multiply_reduce_fusion.2 = (f32[192]{0:T(256)S(1)}, f32[192]{0:T(256)S(1)}, f32[192]{0:T(256)S(1)}, f32[192]{0:T(256)S(1)}, f32[192,4096]{1,0:T(8,128)}, /*index=5*/f32[192,4096]{1,0:T(8,128)}) fusion(bf16[192,8192]{1,0:T(8,128)(2,1)} %bitcast.147, f32[192,4096]{1,0:T(8,128)} %fusion.6, bf16[192,4096]{1,0:T(8,128)(2,1)S(1)} %copy-done.6, ...), kind=kOutput, calls=%fused_computation.18 | convolution fusion | flops 6450315264 | bytes 47713280 | tf_op jit(solution)/shard_map/dot_general | solution.py:62
  116.4 2.4 fusion.14
  120.9 1.5 collective-permute-start
  122.4 65.4 %psum.14 = f32[2,192]{1,0:T(2,128)S(1)} all-reduce(f32[2,192]{1,0:T(2,128)S(1)} %pad_maximum_fusion.1), channel_id=1, replica_groups=mesh['row'=4,'col'=8] {'row','col'}, use_global_device_ids=true, to_apply=%region_4.5 | all-reduce | flops 384 | bytes 3072 | tf_op jit(solution)/shard_map/psum | solution.py:72
  188.0 1.8 fusion.49
  190.8 2.9 collective-permute-start.7
  194.8 3.3 collective-permute-start.3
  198.0 1.5 collective-permute-done.5
  199.6 6.6 %collective-permute-start.2 = (f16[24,4096]{1,0:T(8,128)(2,1)S(1)}, f16[24,4096]{1,0:T(8,128)(2,1)S(1)}, u32[]{:S(2)}, u32[]{:S(2)}) collective-permute-start(f16[24,4096]{1,0:T(8,128)(2,1)S(1)} %get-tuple-element.36), channel_id=1, source_target_pairs={{0,4},{1,5},{2,6},{3,7},{4,0},{5,1},{6,2},{7,3},{8,12},{9,13},{10,... | collective-permute-start | bytes 589832 | tf_op jit(solution)/shard_map/ppermute | solution.py:25
  206.2 12.6 %collective-permute-done.6 = f16[24,4096]{1,0:T(8,128)(2,1)S(1)} collective-permute-done((f16[24,4096]{1,0:T(8,128)(2,1)S(1)}, f16[24,4096]{1,0:T(8,128)(2,1)S(1)}, u32[]{:S(2)}, u32[]{:S(2)}) %collective-permute-start.6) | collective-permute-done | bytes 196640 | tf_op jit(solution)/shard_map/ppermute | solution.py:25
  218.9 7.1 %collective-permute-done.2 = f16[24,4096]{1,0:T(8,128)(2,1)S(1)} collective-permute-done((f16[24,4096]{1,0:T(8,128)(2,1)S(1)}, f16[24,4096]{1,0:T(8,128)(2,1)S(1)}, u32[]{:S(2)}, u32[]{:S(2)}) %collective-permute-start.2) | collective-permute-done | bytes 196640 | tf_op jit(solution)/shard_map/ppermute | solution.py:25
  228.5 13.4 %collective-permute-done.9 = f32[24,4096]{1,0:T(8,128)S(1)} collective-permute-done((f32[24,4096]{1,0:T(8,128)S(1)}, f32[24,4096]{1,0:T(8,128)S(1)}, u32[]{:S(2)}, u32[]{:S(2)}) %collective-permute-start.9) | collective-permute-done | bytes 393248 | tf_op jit(solution)/shard_map/ppermute | solution.py:90
  243.7 5.4 %fusion.12 = f32[8192,128]{1,0:T(8,128)} fusion(f32[192]{0:T(256)S(1)} %bitcast.143, bf16[192,4096]{1,0:T(8,128)(2,1)} %all-gather.7.cloned.1.call-done, bf16[1,192,8192]{2,1,0:T(8,128)(2,1)} %all-gather.11.cloned.1.call-done), kind=kOutput, calls=%fused_computation.20 | convolution fusion | flops 407371776 | bytes 7389952 | tf_op jit(solution)/shard_map/dot_general | solution.py:96
  249.3 32.2 %all-gather.9.cloned.1.call-done = bf16[192,4096]{1,0:T(8,128)(2,1)} async-done(((bf16[48,4096]{1,0:T(8,128)(2,1)}), bf16[192,4096]{1,0:T(8,128)(2,1)}) %all-gather.9.cloned.1.call-update) | async-done | bytes 1572880 | tf_op jit(solution)/shard_map/all_gather | solution.py:54
  281.4 21.3 %fusion.4 = f32[192,4096]{1,0:T(8,128)} fusion(bf16[192,4096]{1,0:T(8,128)(2,1)} %all-gather.9.cloned.1.call-done, bf16[8192,4096]{1,0:T(8,128)(2,1)} %param.5), kind=kOutput, calls=%fused_computation.4 | convolution fusion | flops 6442450944 | bytes 38273024 | tf_op jit(solution)/shard_map/dot_general | solution.py:62
  302.8 41.2 %all-gather.13.cloned.1.call-done = bf16[1,192,8192]{2,1,0:T(8,128)(2,1)} async-done(((bf16[1,24,8192]{2,1,0:T(8,128)(2,1)}), bf16[1,192,8192]{2,1,0:T(8,128)(2,1)}) %all-gather.13.cloned.1.call-update) | async-done | bytes 3145744 | tf_op jit(solution)/shard_map/all_gather | solution.py:59
  344.0 20.1 %multiply_reduce_fusion = (f32[192]{0:T(256)S(1)}, f32[192]{0:T(256)S(1)}, f32[192,4096]{1,0:T(8,128)}, f32[192,4096]{1,0:T(8,128)}) fusion(bf16[192,8192]{1,0:T(8,128)(2,1)} %bitcast.148, f32[192,4096]{1,0:T(8,128)} %fusion.4, f32[192]{0:T(256)S(1)} %multiply_divide_fusion, bf16[192,4096]{1,0:T(8,128)(2,1)S(1)} %copy-done.7, bf16[8192,4096]{1,0:T(8,128)(2,1)} %param.5), kind=kOutput, calls=%fused_computation.16 | convolution fusion | flops 6448742400 | bytes 47712512 | tf_op jit(solution)/shard_map/dot_general | solution.py:62
  364.1 39.2 %psum.15 = f32[192]{0:T(256)S(1)} all-reduce(f32[192]{0:T(256)S(1)} %add.236), channel_id=1, replica_groups=mesh['row'=4,'col'=8] {'row','col'}, use_global_device_ids=true, to_apply=%region_7.8 | all-reduce | flops 192 | bytes 1536 | tf_op jit(solution)/shard_map/psum | solution.py:75
  403.3 1.6 fusion.15
  406.5 2.3 collective-permute-start.14
  408.9 6.6 %fusion.9 = f32[8192,128]{1,0:T(8,128)} fusion(f32[8192,128]{1,0:T(8,128)} %fusion.12, f32[192]{0:T(256)S(1)} %psum.15, bf16[8192,4096]{1,0:T(8,128)(2,1)} %param.5, bf16[192,4096]{1,0:T(8,128)(2,1)S(1)} %copy-done.7, bf16[1,192,8192]{2,1,0:T(8,128)(2,1)S(1)} %copy-done.5), kind=kOutput, calls=%fused_computation.10 | convolution fusion | flops 411566080 | bytes 13681664 | tf_op jit(solution)/shard_map/dot_general | solution.py:96
  415.6 11.8 %collective-permute-done.14 = f16[4,24,4096]{2,1,0:T(8,128)(2,1)S(1)} collective-permute-done((f16[4,24,4096]{2,1,0:T(8,128)(2,1)S(1)}, f16[4,24,4096]{2,1,0:T(8,128)(2,1)S(1)}, u32[]{:S(2)}, u32[]{:S(2)}) %collective-permute-start.14) | collective-permute-done | bytes 786464 | tf_op jit(solution)/shard_map/ppermute | solution.py:18
  428.3 3.2 collective-permute-start.17
  431.6 10.9 %collective-permute-done.10 = f16[4,24,4096]{2,1,0:T(8,128)(2,1)S(1)} collective-permute-done((f16[4,24,4096]{2,1,0:T(8,128)(2,1)S(1)}, f16[4,24,4096]{2,1,0:T(8,128)(2,1)S(1)}, u32[]{:S(2)}, u32[]{:S(2)}) %collective-permute-start.10) | collective-permute-done | bytes 786464 | tf_op jit(solution)/shard_map/ppermute | solution.py:18
  443.5 3.3 collective-permute-start.13
  446.9 5.7 %collective-permute-done.11 = f16[24,4096]{1,0:T(8,128)(2,1)S(1)} collective-permute-done((f16[24,4096]{1,0:T(8,128)(2,1)S(1)}, f16[24,4096]{1,0:T(8,128)(2,1)S(1)}, u32[]{:S(2)}, u32[]{:S(2)}) %collective-permute-start.11) | collective-permute-done | bytes 196640 | tf_op jit(solution)/shard_map/ppermute | solution.py:25
  453.5 8.0 %collective-permute-done.12 = f16[24,4096]{1,0:T(8,128)(2,1)S(1)} collective-permute-done((f16[24,4096]{1,0:T(8,128)(2,1)S(1)}, f16[24,4096]{1,0:T(8,128)(2,1)S(1)}, u32[]{:S(2)}, u32[]{:S(2)}) %collective-permute-start.12) | collective-permute-done | bytes 196640 | tf_op jit(solution)/shard_map/ppermute | solution.py:25
  (76 shorter events, 16.1 us)
Async XLA Ops:
  7.2 1.2 copy-start
  7.2 25.9 %all-gather.7.cloned.1.call-start = ((), (), s32[]{:S(2)}) async-start(), calls=%async_computation | async-start | bytes 1966080 | tf_op jit(solution)/shard_map/all_gather | solution.py:54
  10.6 85.7 %all-gather.11.cloned.1.call-start = ((), (), s32[]{:S(2)}) async-start(), calls=%async_computation.2 | async-start | bytes 3538944 | tf_op jit(solution)/shard_map/all_gather | solution.py:41
  12.7 268.8 %all-gather.9.cloned.1.call-start = ((), (), s32[]{:S(2)}) async-start(), calls=%async_computation.1 | async-start | bytes 1966080 | tf_op jit(solution)/shard_map/all_gather | solution.py:54
  33.1 63.2 %copy-start.6 = (bf16[192,4096]{1,0:T(8,128)(2,1)S(1)}, bf16[192,4096]{1,0:T(8,128)(2,1)}, u32[]{:S(2)}) copy-start(bf16[192,4096]{1,0:T(8,128)(2,1)} %all-gather.7.cloned.1.call-done) | copy-start | bytes 4718596
  118.8 69.1 %collective-permute-start.4 = (f16[4,24,4096]{2,1,0:T(8,128)(2,1)}, f16[4,24,4096]{2,1,0:T(8,128)(2,1)S(1)}, u32[]{:S(2)}, u32[]{:S(2)}) collective-permute-start(f16[4,24,4096]{2,1,0:T(8,128)(2,1)} %fusion.14), channel_id=1, source_target_pairs={{0,1},{1,0},{2,3},{3,2},{4,5},{5,4},{6,7},{7,6},{8,9},{9,8},{10,11... | collective-permute-start | bytes 2359304 | tf_op jit(solution)/shard_map/ppermute | solution.py:18
  120.9 72.9 %collective-permute-start = (f16[4,24,4096]{2,1,0:T(8,128)(2,1)S(1)}, f16[4,24,4096]{2,1,0:T(8,128)(2,1)S(1)}, u32[]{:S(2)}, u32[]{:S(2)}) collective-permute-start(f16[4,24,4096]{2,1,0:T(8,128)(2,1)S(1)} %fusion.13), channel_id=1, source_target_pairs={{0,1},{1,0},{2,3},{3,2},{4,5},{5,4},{6,7},{7,6},{8,9},{9,8},{10,11... | collective-permute-start | bytes 2359304 | tf_op jit(solution)/shard_map/ppermute | solution.py:18
  187.9 5.9 %copy-start.2 = (f32[192,4096]{1,0:T(8,128)S(1)}, f32[192,4096]{1,0:T(8,128)}, u32[]{:S(2)}) copy-start(f32[192,4096]{1,0:T(8,128)} %get-tuple-element.18) | copy-start | bytes 9437188
  189.9 9.7 %collective-permute-start.5 = (f16[24,4096]{1,0:T(8,128)(2,1)S(1)}, f16[24,4096]{1,0:T(8,128)(2,1)S(1)}, u32[]{:S(2)}, u32[]{:S(2)}) collective-permute-start(f16[24,4096]{1,0:T(8,128)(2,1)S(1)} %get-tuple-element.37), channel_id=1, source_target_pairs={{0,2},{1,3},{2,4},{3,5},{4,6},{5,7},{6,0},{7,1},{8,10},{9,11},{10,... | collective-permute-start | bytes 589832 | tf_op jit(solution)/shard_map/ppermute | solution.py:25
  190.8 15.3 %collective-permute-start.7 = (f16[24,4096]{1,0:T(8,128)(2,1)S(1)}, f16[24,4096]{1,0:T(8,128)(2,1)S(1)}, u32[]{:S(2)}, u32[]{:S(2)}) collective-permute-start(f16[24,4096]{1,0:T(8,128)(2,1)S(1)} %get-tuple-element.38), channel_id=1, source_target_pairs={{0,6},{1,7},{2,0},{3,1},{4,2},{5,3},{6,4},{7,5},{8,14},{9,15},{10,... | collective-permute-start | bytes 589832 | tf_op jit(solution)/shard_map/ppermute | solution.py:25
  193.8 25.0 %collective-permute-start.6 = (f16[24,4096]{1,0:T(8,128)(2,1)S(1)}, f16[24,4096]{1,0:T(8,128)(2,1)S(1)}, u32[]{:S(2)}, u32[]{:S(2)}) collective-permute-start(f16[24,4096]{1,0:T(8,128)(2,1)S(1)} %get-tuple-element.39), channel_id=1, source_target_pairs={{0,4},{1,5},{2,6},{3,7},{4,0},{5,1},{6,2},{7,3},{8,12},{9,13},{10,... | collective-permute-start | bytes 589832 | tf_op jit(solution)/shard_map/ppermute | solution.py:25
  194.2 24.7 %collective-permute-start.1 = (f16[24,4096]{1,0:T(8,128)(2,1)S(1)}, f16[24,4096]{1,0:T(8,128)(2,1)S(1)}, u32[]{:S(2)}, u32[]{:S(2)}) collective-permute-start(f16[24,4096]{1,0:T(8,128)(2,1)S(1)} %get-tuple-element.34), channel_id=1, source_target_pairs={{0,2},{1,3},{2,4},{3,5},{4,6},{5,7},{6,0},{7,1},{8,10},{9,11},{10,... | collective-permute-start | bytes 589832 | tf_op jit(solution)/shard_map/ppermute | solution.py:25
  194.8 24.1 %collective-permute-start.3 = (f16[24,4096]{1,0:T(8,128)(2,1)S(1)}, f16[24,4096]{1,0:T(8,128)(2,1)S(1)}, u32[]{:S(2)}, u32[]{:S(2)}) collective-permute-start(f16[24,4096]{1,0:T(8,128)(2,1)S(1)} %get-tuple-element.35), channel_id=1, source_target_pairs={{0,6},{1,7},{2,0},{3,1},{4,2},{5,3},{6,4},{7,5},{8,14},{9,15},{10,... | collective-permute-start | bytes 589832 | tf_op jit(solution)/shard_map/ppermute | solution.py:25
  199.6 26.4 %collective-permute-start.2 = (f16[24,4096]{1,0:T(8,128)(2,1)S(1)}, f16[24,4096]{1,0:T(8,128)(2,1)S(1)}, u32[]{:S(2)}, u32[]{:S(2)}) collective-permute-start(f16[24,4096]{1,0:T(8,128)(2,1)S(1)} %get-tuple-element.36), channel_id=1, source_target_pairs={{0,4},{1,5},{2,6},{3,7},{4,0},{5,1},{6,2},{7,3},{8,12},{9,13},{10,... | collective-permute-start | bytes 589832 | tf_op jit(solution)/shard_map/ppermute | solution.py:25
  226.2 15.6 %collective-permute-start.9 = (f32[24,4096]{1,0:T(8,128)S(1)}, f32[24,4096]{1,0:T(8,128)S(1)}, u32[]{:S(2)}, u32[]{:S(2)}) collective-permute-start(f32[24,4096]{1,0:T(8,128)S(1)} %get-tuple-element.32), channel_id=1, source_target_pairs={{0,1},{1,0},{2,9},{3,8},{4,17},{5,16},{6,25},{7,24},{8,3},{9,2},{1... | collective-permute-start | bytes 1179656 | tf_op jit(solution)/shard_map/ppermute | solution.py:90
  227.7 14.2 %collective-permute-start.8 = (f32[24,4096]{1,0:T(8,128)S(1)}, f32[24,4096]{1,0:T(8,128)S(1)}, u32[]{:S(2)}, u32[]{:S(2)}) collective-permute-start(f32[24,4096]{1,0:T(8,128)S(1)} %get-tuple-element.33), channel_id=1, source_target_pairs={{0,0},{1,1},{2,8},{3,9},{4,16},{5,17},{6,24},{7,25},{8,2},{9,3},{1... | collective-permute-start | bytes 1179656 | tf_op jit(solution)/shard_map/ppermute | solution.py:90
  243.1 100.8 %all-gather.13.cloned.1.call-start = ((), (), s32[]{:S(2)}) async-start(), calls=%async_computation.3 | async-start | bytes 3538944 | tf_op jit(solution)/shard_map/all_gather | solution.py:59
  281.4 62.5 %copy-start.7 = (bf16[192,4096]{1,0:T(8,128)(2,1)S(1)}, bf16[192,4096]{1,0:T(8,128)(2,1)}, u32[]{:S(2)}) copy-start(bf16[192,4096]{1,0:T(8,128)(2,1)} %all-gather.9.cloned.1.call-done) | copy-start | bytes 4718596
  403.3 5.7 %copy-start.5 = (bf16[1,192,8192]{2,1,0:T(8,128)(2,1)S(1)}, bf16[1,192,8192]{2,1,0:T(8,128)(2,1)}, u32[]{:S(2)}) copy-start(bf16[1,192,8192]{2,1,0:T(8,128)(2,1)} %all-gather.13.cloned.1.call-done) | copy-start | bytes 9437188
  406.5 20.8 %copy-start.4 = (f32[192,4096]{1,0:T(8,128)S(1)}, f32[192,4096]{1,0:T(8,128)}, u32[]{:S(2)}) copy-start(f32[192,4096]{1,0:T(8,128)} %get-tuple-element.17) | copy-start | bytes 9437188
  406.5 20.8 %collective-permute-start.14 = (f16[4,24,4096]{2,1,0:T(8,128)(2,1)S(1)}, f16[4,24,4096]{2,1,0:T(8,128)(2,1)S(1)}, u32[]{:S(2)}, u32[]{:S(2)}) collective-permute-start(f16[4,24,4096]{2,1,0:T(8,128)(2,1)S(1)} %fusion.16), channel_id=1, source_target_pairs={{0,1},{1,0},{2,3},{3,2},{4,5},{5,4},{6,7},{7,6},{8,9},{9,8},{10,11... | collective-permute-start | bytes 2359304 | tf_op jit(solution)/shard_map/ppermute | solution.py:18
  408.9 33.6 %collective-permute-start.10 = (f16[4,24,4096]{2,1,0:T(8,128)(2,1)S(1)}, f16[4,24,4096]{2,1,0:T(8,128)(2,1)S(1)}, u32[]{:S(2)}, u32[]{:S(2)}) collective-permute-start(f16[4,24,4096]{2,1,0:T(8,128)(2,1)S(1)} %fusion.15), channel_id=1, source_target_pairs={{0,1},{1,0},{2,3},{3,2},{4,5},{5,4},{6,7},{7,6},{8,9},{9,8},{10,11... | collective-permute-start | bytes 2359304 | tf_op jit(solution)/shard_map/ppermute | solution.py:18
  415.6 26.9 %copy-start.3 = (f32[192,4096]{1,0:T(8,128)S(1)}, f32[192,4096]{1,0:T(8,128)}, u32[]{:S(2)}) copy-start(f32[192,4096]{1,0:T(8,128)} %get-tuple-element.16) | copy-start | bytes 9437188
  427.7 19.1 %collective-permute-start.15 = (f16[24,4096]{1,0:T(8,128)(2,1)S(1)}, f16[24,4096]{1,0:T(8,128)(2,1)S(1)}, u32[]{:S(2)}, u32[]{:S(2)}) collective-permute-start(f16[24,4096]{1,0:T(8,128)(2,1)S(1)} %get-tuple-element.29), channel_id=1, source_target_pairs={{0,2},{1,3},{2,4},{3,5},{4,6},{5,7},{6,0},{7,1},{8,10},{9,11},{10,... | collective-permute-start | bytes 589832 | tf_op jit(solution)/shard_map/ppermute | solution.py:25
  428.3 18.4 %collective-permute-start.17 = (f16[24,4096]{1,0:T(8,128)(2,1)S(1)}, f16[24,4096]{1,0:T(8,128)(2,1)S(1)}, u32[]{:S(2)}, u32[]{:S(2)}) collective-permute-start(f16[24,4096]{1,0:T(8,128)(2,1)S(1)} %get-tuple-element.30), channel_id=1, source_target_pairs={{0,6},{1,7},{2,0},{3,1},{4,2},{5,3},{6,4},{7,5},{8,14},{9,15},{10,... | collective-permute-start | bytes 589832 | tf_op jit(solution)/shard_map/ppermute | solution.py:25
  431.6 15.2 %collective-permute-start.16 = (f16[24,4096]{1,0:T(8,128)(2,1)S(1)}, f16[24,4096]{1,0:T(8,128)(2,1)S(1)}, u32[]{:S(2)}, u32[]{:S(2)}) collective-permute-start(f16[24,4096]{1,0:T(8,128)(2,1)S(1)} %get-tuple-element.31), channel_id=1, source_target_pairs={{0,4},{1,5},{2,6},{3,7},{4,0},{5,1},{6,2},{7,3},{8,12},{9,13},{10,... | collective-permute-start | bytes 589832 | tf_op jit(solution)/shard_map/ppermute | solution.py:25
  442.9 9.7 %collective-permute-start.11 = (f16[24,4096]{1,0:T(8,128)(2,1)S(1)}, f16[24,4096]{1,0:T(8,128)(2,1)S(1)}, u32[]{:S(2)}, u32[]{:S(2)}) collective-permute-start(f16[24,4096]{1,0:T(8,128)(2,1)S(1)} %get-tuple-element.26), channel_id=1, source_target_pairs={{0,2},{1,3},{2,4},{3,5},{4,6},{5,7},{6,0},{7,1},{8,10},{9,11},{10,... | collective-permute-start | bytes 589832 | tf_op jit(solution)/shard_map/ppermute | solution.py:25
  443.5 10.0 %collective-permute-start.13 = (f16[24,4096]{1,0:T(8,128)(2,1)S(1)}, f16[24,4096]{1,0:T(8,128)(2,1)S(1)}, u32[]{:S(2)}, u32[]{:S(2)}) collective-permute-start(f16[24,4096]{1,0:T(8,128)(2,1)S(1)} %get-tuple-element.27), channel_id=1, source_target_pairs={{0,6},{1,7},{2,0},{3,1},{4,2},{5,3},{6,4},{7,5},{8,14},{9,15},{10,... | collective-permute-start | bytes 589832 | tf_op jit(solution)/shard_map/ppermute | solution.py:25
  446.8 14.7 %collective-permute-start.12 = (f16[24,4096]{1,0:T(8,128)(2,1)S(1)}, f16[24,4096]{1,0:T(8,128)(2,1)S(1)}, u32[]{:S(2)}, u32[]{:S(2)}) collective-permute-start(f16[24,4096]{1,0:T(8,128)(2,1)S(1)} %get-tuple-element.28), channel_id=1, source_target_pairs={{0,4},{1,5},{2,6},{3,7},{4,0},{5,1},{6,2},{7,3},{8,12},{9,13},{10,... | collective-permute-start | bytes 589832 | tf_op jit(solution)/shard_map/ppermute | solution.py:25
  446.8 16.2 %copy-start.1 = (bf16[96,4096]{1,0:T(8,128)(2,1)S(1)}, bf16[96,4096]{1,0:T(8,128)(2,1)}, u32[]{:S(2)}) copy-start(bf16[96,4096]{1,0:T(8,128)(2,1)} %param.6) | copy-start | bytes 2359300
Sparse Core Ops, SparseCore 0:
  10.7 22.3 all-gather.6
  35.8 60.4 all-gather.10
  243.3 38.1 all-gather.8
  283.5 60.4 all-gather.12
where the time goes:
time: 470 us; the launch traced here: 469 us
  waiting for transfers between devices  208 us (44%)
  blocking collectives  105 us (22%)
  matrix products  98.1 us (21%)
  starting transfers between devices  29 us (6%)
  between operations  14.1 us (3%)
  other arithmetic  11.9 us (3%)
    dot_general x4, matrix products, on_device(): lax.dot_general(weighted_back, transition[rows], (((1,), (1,)), ((), ()))...  82.8 us
    psum x1, blocking collectives, on_device(): both = lax.psum(jnp.stack([norm, mass]), ('row', 'col'))  65.4 us
    all_gather x2, waiting for transfers between devices, on_device(): weighted_back = lax.all_gather(local_back, 'row', axis=0, tiled=True)  52.4 us
    all_gather x1, waiting for transfers between devices, on_device(): forward_all = [None, lax.all_gather(forward[1], 'col', axis=0, tiled=True)]  42 us
    all_gather x1, waiting for transfers between devices, on_device(): forward_all[0] = lax.all_gather(forward[0], 'col', axis=0, tiled=True)  41.2 us
    psum x1, blocking collectives, on_device(): normal_all = lax.psum(norm, ('row', 'col'))  39.2 us
    ppermute x12, waiting for transfers between devices, reduce_scatter(): lax.ppermute(piece, 'col', [(c, (c + 2 * k) % col_count) for c in range(c...  35.8 us
    ppermute x4, waiting for transfers between devices, reduce_scatter(): got = lax.ppermute(away, 'col', [(c, c ^ 1) for c in range(col_count)])  22.7 us
  transfers between devices with their start and end apart: 22, of which 13 were waited for; matrix products, arithmetic and copies ran while one was open for 13% of the time, Pallas kernels for 0%

commit v1 on v0

--- a/solution.py
+++ b/solution.py
@@ -69,7 +69,7 @@
             mass = mass + jnp.sum(partial, axis=1)
             pieces.append(reduce_scatter(partial, scale, col_count, col_index, local_seqs))
         if step == 1:
-            both = lax.psum(jnp.stack([norm, mass]), ("row", "col"))
+            both = lax.psum(lax.psum(jnp.stack([norm, mass]), "col"), "row")
             normal_all = both[0]
         else:
             normal_all = lax.psum(norm, ("row", "col"))

time: 470 us -> 454 us (0.966)
  blocking collectives: 105 us -> 89.3 us
  waiting for transfers between devices: 208 us -> 215 us
  starting transfers between devices: 29 us -> 22.1 us
    psum x1 -> x2, blocking collectives: 65.4 us -> 50.1 us  [on_device(): both = lax.psum(lax.psum(jnp.stack([norm, mass]), 'col'), 'row')]
    ppermute x12, starting transfers between devices: 22.1 us -> 15.5 us  [reduce_scatter(): lax.ppermute(piece, 'col', [(c, (c + 2 * k) % col_count) for c in range(c...]
    ppermute x12, waiting for transfers between devices: 35.8 us -> 40.9 us  [reduce_scatter(): lax.ppermute(piece, 'col', [(c, (c + 2 * k) % col_count) for c in range(c...]
  transfers between devices with their start and end apart: 22 -> 22, of which waited for: 13 -> 15; matrix products, arithmetic and copies ran while one was open for 13% -> 14% of each run, Pallas kernels for 0% -> 0%
where the time goes in v1:
time: 454 us
  waiting for transfers between devices  215 us (47%)
  matrix products  98.2 us (22%)
  blocking collectives  89.3 us (20%)
  starting transfers between devices  22.1 us (5%)
  between operations  14.1 us (3%)
  other arithmetic  11.9 us (3%)
    dot_general x4, matrix products, on_device(): lax.dot_general(weighted_back, transition[rows], (((1,), (1,)), ((), ()))...  82.9 us
    all_gather x2, waiting for transfers between devices, on_device(): weighted_back = lax.all_gather(local_back, 'row', axis=0, tiled=True)  53 us
    psum x2, blocking collectives, on_device(): both = lax.psum(lax.psum(jnp.stack([norm, mass]), 'col'), 'row')  50.1 us
    all_gather x1, waiting for transfers between devices, on_device(): forward_all = [None, lax.all_gather(forward[1], 'col', axis=0, tiled=True)]  42 us
    all_gather x1, waiting for transfers between devices, on_device(): forward_all[0] = lax.all_gather(forward[0], 'col', axis=0, tiled=True)  41.1 us
    ppermute x12, waiting for transfers between devices, reduce_scatter(): lax.ppermute(piece, 'col', [(c, (c + 2 * k) % col_count) for c in range(c...  40.9 us
    psum x1, blocking collectives, on_device(): normal_all = lax.psum(norm, ('row', 'col'))  39.2 us
    ppermute x4, waiting for transfers between devices, reduce_scatter(): got = lax.ppermute(away, 'col', [(c, c ^ 1) for c in range(col_count)])  22.7 us
  transfers between devices with their start and end apart: 22, of which 15 were waited for; matrix products, arithmetic and copies ran while one was open for 14% of the time, Pallas kernels for 0%

profile of v1, /device:TPU:0, one launch (start us, length us, event | category | flops | bytes accessed | tf_op | source)
XLA Modules:
  0.0 453.9 jit_solution(10848012479626981116)
XLA Ops:
  8.3 2.2 fusion.10
  10.6 2.0 fusion.50
  12.8 20.2 %all-gather.7.cloned.1.call-done = bf16[192,4096]{1,0:T(8,128)(2,1)} async-done(((bf16[48,4096]{1,0:T(8,128)(2,1)}), bf16[192,4096]{1,0:T(8,128)(2,1)}) %all-gather.7.cloned.1.call-update) | async-done | bytes 1572880 | tf_op jit(solution)/shard_map/all_gather | solution.py:54
  33.1 21.2 %fusion.6 = f32[192,4096]{1,0:T(8,128)} fusion(bf16[192,4096]{1,0:T(8,128)(2,1)} %all-gather.7.cloned.1.call-done, bf16[8192,4096]{1,0:T(8,128)(2,1)} %param.5), kind=kOutput, calls=%fused_computation.6 | convolution fusion | flops 6442450944 | bytes 38273024 | tf_op jit(solution)/shard_map/dot_general | solution.py:62
  54.3 42.0 %all-gather.11.cloned.1.call-done = bf16[1,192,8192]{2,1,0:T(8,128)(2,1)} async-done(((bf16[1,24,8192]{2,1,0:T(8,128)(2,1)}), bf16[1,192,8192]{2,1,0:T(8,128)(2,1)}) %all-gather.11.cloned.1.call-update) | async-done | bytes 3145744 | tf_op jit(solution)/shard_map/all_gather | solution.py:41
  96.3 20.1 %multiply_reduce_fusion.2 = (f32[192]{0:T(256)S(1)}, f32[192]{0:T(256)S(1)}, f32[192]{0:T(256)S(1)}, f32[192]{0:T(256)S(1)}, f32[192,4096]{1,0:T(8,128)}, /*index=5*/f32[192,4096]{1,0:T(8,128)}) fusion(bf16[192,8192]{1,0:T(8,128)(2,1)} %bitcast.147, f32[192,4096]{1,0:T(8,128)} %fusion.6, bf16[192,4096]{1,0:T(8,128)(2,1)S(1)} %copy-done.6, ...), kind=kOutput, calls=%fused_computation.18 | convolution fusion | flops 6450315264 | bytes 47713280 | tf_op jit(solution)/shard_map/dot_general | solution.py:62
  116.4 2.4 fusion.14
  120.8 1.5 collective-permute-start
  122.4 44.4 %psum.21 = f32[2,192]{1,0:T(2,128)S(1)} all-reduce(f32[2,192]{1,0:T(2,128)S(1)} %pad_maximum_fusion.1), channel_id=1, replica_groups=mesh['row'=4,'col'=8] {'col'}, use_global_device_ids=true, to_apply=%region_4.5 | all-reduce | flops 384 | bytes 3072 | tf_op jit(solution)/shard_map/psum | solution.py:72
  166.8 5.6 %psum.22 = f32[2,192]{1,0:T(2,128)S(1)} all-reduce(f32[2,192]{1,0:T(2,128)S(1)} %psum.21), channel_id=1, replica_groups=mesh['row'=4,'col'=8] {'row'}, use_global_device_ids=true, to_apply=%region_5.6 | all-reduce | flops 384 | bytes 3072 | tf_op jit(solution)/shard_map/psum | solution.py:72
  172.6 1.8 fusion.49
  174.6 3.8 collective-permute-start.7
  179.4 3.3 collective-permute-start.3
  184.1 6.2 %collective-permute-done.7 = f16[24,4096]{1,0:T(8,128)(2,1)S(1)} collective-permute-done((f16[24,4096]{1,0:T(8,128)(2,1)S(1)}, f16[24,4096]{1,0:T(8,128)(2,1)S(1)}, u32[]{:S(2)}, u32[]{:S(2)}) %collective-permute-start.7) | collective-permute-done | bytes 196640 | tf_op jit(solution)/shard_map/ppermute | solution.py:25
  190.3 6.6 %collective-permute-done.6 = f16[24,4096]{1,0:T(8,128)(2,1)S(1)} collective-permute-done((f16[24,4096]{1,0:T(8,128)(2,1)S(1)}, f16[24,4096]{1,0:T(8,128)(2,1)S(1)}, u32[]{:S(2)}, u32[]{:S(2)}) %collective-permute-start.6) | collective-permute-done | bytes 196640 | tf_op jit(solution)/shard_map/ppermute | solution.py:25
  198.1 10.9 %collective-permute-done.2 = f16[24,4096]{1,0:T(8,128)(2,1)S(1)} collective-permute-done((f16[24,4096]{1,0:T(8,128)(2,1)S(1)}, f16[24,4096]{1,0:T(8,128)(2,1)S(1)}, u32[]{:S(2)}, u32[]{:S(2)}) %collective-permute-start.2) | collective-permute-done | bytes 196640 | tf_op jit(solution)/shard_map/ppermute | solution.py:25
  211.1 14.5 %collective-permute-done.9 = f32[24,4096]{1,0:T(8,128)S(1)} collective-permute-done((f32[24,4096]{1,0:T(8,128)S(1)}, f32[24,4096]{1,0:T(8,128)S(1)}, u32[]{:S(2)}, u32[]{:S(2)}) %collective-permute-start.9) | collective-permute-done | bytes 393248 | tf_op jit(solution)/shard_map/ppermute | solution.py:90
  227.4 5.4 %fusion.12 = f32[8192,128]{1,0:T(8,128)} fusion(f32[192]{0:T(256)S(1)} %bitcast.143, bf16[192,4096]{1,0:T(8,128)(2,1)} %all-gather.7.cloned.1.call-done, bf16[1,192,8192]{2,1,0:T(8,128)(2,1)} %all-gather.11.cloned.1.call-done), kind=kOutput, calls=%fused_computation.20 | convolution fusion | flops 407371776 | bytes 7389952 | tf_op jit(solution)/shard_map/dot_general | solution.py:96
  233.0 32.8 %all-gather.9.cloned.1.call-done = bf16[192,4096]{1,0:T(8,128)(2,1)} async-done(((bf16[48,4096]{1,0:T(8,128)(2,1)}), bf16[192,4096]{1,0:T(8,128)(2,1)}) %all-gather.9.cloned.1.call-update) | async-done | bytes 1572880 | tf_op jit(solution)/shard_map/all_gather | solution.py:54
  265.8 21.4 %fusion.4 = f32[192,4096]{1,0:T(8,128)} fusion(bf16[192,4096]{1,0:T(8,128)(2,1)} %all-gather.9.cloned.1.call-done, bf16[8192,4096]{1,0:T(8,128)(2,1)} %param.5), kind=kOutput, calls=%fused_computation.4 | convolution fusion | flops 6442450944 | bytes 38273024 | tf_op jit(solution)/shard_map/dot_general | solution.py:62
  287.2 41.1 %all-gather.13.cloned.1.call-done = bf16[1,192,8192]{2,1,0:T(8,128)(2,1)} async-done(((bf16[1,24,8192]{2,1,0:T(8,128)(2,1)}), bf16[1,192,8192]{2,1,0:T(8,128)(2,1)}) %all-gather.13.cloned.1.call-update) | async-done | bytes 3145744 | tf_op jit(solution)/shard_map/all_gather | solution.py:59
  328.3 20.2 %multiply_reduce_fusion = (f32[192]{0:T(256)S(1)}, f32[192]{0:T(256)S(1)}, f32[192,4096]{1,0:T(8,128)}, f32[192,4096]{1,0:T(8,128)}) fusion(bf16[192,8192]{1,0:T(8,128)(2,1)} %bitcast.148, f32[192,4096]{1,0:T(8,128)} %fusion.4, f32[192]{0:T(256)S(1)} %multiply_divide_fusion, bf16[192,4096]{1,0:T(8,128)(2,1)S(1)} %copy-done.7, bf16[8192,4096]{1,0:T(8,128)(2,1)} %param.5), kind=kOutput, calls=%fused_computation.16 | convolution fusion | flops 6448742400 | bytes 47712512 | tf_op jit(solution)/shard_map/dot_general | solution.py:62
  348.5 39.2 %psum.23 = f32[192]{0:T(256)S(1)} all-reduce(f32[192]{0:T(256)S(1)} %add.238), channel_id=1, replica_groups=mesh['row'=4,'col'=8] {'row','col'}, use_global_device_ids=true, to_apply=%region_8.9 | all-reduce | flops 192 | bytes 1536 | tf_op jit(solution)/shard_map/psum | solution.py:75
  387.7 1.6 fusion.15
  390.9 2.3 collective-permute-start.14
  393.3 6.6 %fusion.9 = f32[8192,128]{1,0:T(8,128)} fusion(f32[8192,128]{1,0:T(8,128)} %fusion.12, f32[192]{0:T(256)S(1)} %psum.23, bf16[8192,4096]{1,0:T(8,128)(2,1)} %param.5, bf16[192,4096]{1,0:T(8,128)(2,1)S(1)} %copy-done.7, bf16[1,192,8192]{2,1,0:T(8,128)(2,1)S(1)} %copy-done.5), kind=kOutput, calls=%fused_computation.10 | convolution fusion | flops 411566080 | bytes 13681664 | tf_op jit(solution)/shard_map/dot_general | solution.py:96
  400.0 11.7 %collective-permute-done.14 = f16[4,24,4096]{2,1,0:T(8,128)(2,1)S(1)} collective-permute-done((f16[4,24,4096]{2,1,0:T(8,128)(2,1)S(1)}, f16[4,24,4096]{2,1,0:T(8,128)(2,1)S(1)}, u32[]{:S(2)}, u32[]{:S(2)}) %collective-permute-start.14) | collective-permute-done | bytes 786464 | tf_op jit(solution)/shard_map/ppermute | solution.py:18
  412.7 3.2 collective-permute-start.17
  416.0 10.9 %collective-permute-done.10 = f16[4,24,4096]{2,1,0:T(8,128)(2,1)S(1)} collective-permute-done((f16[4,24,4096]{2,1,0:T(8,128)(2,1)S(1)}, f16[4,24,4096]{2,1,0:T(8,128)(2,1)S(1)}, u32[]{:S(2)}, u32[]{:S(2)}) %collective-permute-start.10) | collective-permute-done | bytes 786464 | tf_op jit(solution)/shard_map/ppermute | solution.py:18
  427.9 3.3 collective-permute-start.13
  431.3 5.7 %collective-permute-done.11 = f16[24,4096]{1,0:T(8,128)(2,1)S(1)} collective-permute-done((f16[24,4096]{1,0:T(8,128)(2,1)S(1)}, f16[24,4096]{1,0:T(8,128)(2,1)S(1)}, u32[]{:S(2)}, u32[]{:S(2)}) %collective-permute-start.11) | collective-permute-done | bytes 196640 | tf_op jit(solution)/shard_map/ppermute | solution.py:25
  437.9 8.0 %collective-permute-done.12 = f16[24,4096]{1,0:T(8,128)(2,1)S(1)} collective-permute-done((f16[24,4096]{1,0:T(8,128)(2,1)S(1)}, f16[24,4096]{1,0:T(8,128)(2,1)S(1)}, u32[]{:S(2)}, u32[]{:S(2)}) %collective-permute-start.12) | collective-permute-done | bytes 196640 | tf_op jit(solution)/shard_map/ppermute | solution.py:25
  (77 shorter events, 17.4 us)
Async XLA Ops:
  7.2 1.2 copy-start
  7.2 25.9 %all-gather.7.cloned.1.call-start = ((), (), s32[]{:S(2)}) async-start(), calls=%async_computation | async-start | bytes 1966080 | tf_op jit(solution)/shard_map/all_gather | solution.py:54
  10.6 85.7 %all-gather.11.cloned.1.call-start = ((), (), s32[]{:S(2)}) async-start(), calls=%async_computation.2 | async-start | bytes 3538944 | tf_op jit(solution)/shard_map/all_gather | solution.py:41
  12.7 253.1 %all-gather.9.cloned.1.call-start = ((), (), s32[]{:S(2)}) async-start(), calls=%async_computation.1 | async-start | bytes 1966080 | tf_op jit(solution)/shard_map/all_gather | solution.py:54
  33.1 63.2 %copy-start.6 = (bf16[192,4096]{1,0:T(8,128)(2,1)S(1)}, bf16[192,4096]{1,0:T(8,128)(2,1)}, u32[]{:S(2)}) copy-start(bf16[192,4096]{1,0:T(8,128)(2,1)} %all-gather.7.cloned.1.call-done) | copy-start | bytes 4718596
  118.8 53.8 %collective-permute-start.4 = (f16[4,24,4096]{2,1,0:T(8,128)(2,1)}, f16[4,24,4096]{2,1,0:T(8,128)(2,1)S(1)}, u32[]{:S(2)}, u32[]{:S(2)}) collective-permute-start(f16[4,24,4096]{2,1,0:T(8,128)(2,1)} %fusion.14), channel_id=1, source_target_pairs={{0,1},{1,0},{2,3},{3,2},{4,5},{5,4},{6,7},{7,6},{8,9},{9,8},{10,11... | collective-permute-start | bytes 2359304 | tf_op jit(solution)/shard_map/ppermute | solution.py:18
  120.8 57.5 %collective-permute-start = (f16[4,24,4096]{2,1,0:T(8,128)(2,1)S(1)}, f16[4,24,4096]{2,1,0:T(8,128)(2,1)S(1)}, u32[]{:S(2)}, u32[]{:S(2)}) collective-permute-start(f16[4,24,4096]{2,1,0:T(8,128)(2,1)S(1)} %fusion.13), channel_id=1, source_target_pairs={{0,1},{1,0},{2,3},{3,2},{4,5},{5,4},{6,7},{7,6},{8,9},{9,8},{10,11... | collective-permute-start | bytes 2359304 | tf_op jit(solution)/shard_map/ppermute | solution.py:18
  172.5 5.9 %copy-start.2 = (f32[192,4096]{1,0:T(8,128)S(1)}, f32[192,4096]{1,0:T(8,128)}, u32[]{:S(2)}) copy-start(f32[192,4096]{1,0:T(8,128)} %get-tuple-element.18) | copy-start | bytes 9437188
  174.5 9.6 %collective-permute-start.5 = (f16[24,4096]{1,0:T(8,128)(2,1)S(1)}, f16[24,4096]{1,0:T(8,128)(2,1)S(1)}, u32[]{:S(2)}, u32[]{:S(2)}) collective-permute-start(f16[24,4096]{1,0:T(8,128)(2,1)S(1)} %get-tuple-element.37), channel_id=1, source_target_pairs={{0,2},{1,3},{2,4},{3,5},{4,6},{5,7},{6,0},{7,1},{8,10},{9,11},{10,... | collective-permute-start | bytes 589832 | tf_op jit(solution)/shard_map/ppermute | solution.py:25
  174.6 15.7 %collective-permute-start.7 = (f16[24,4096]{1,0:T(8,128)(2,1)S(1)}, f16[24,4096]{1,0:T(8,128)(2,1)S(1)}, u32[]{:S(2)}, u32[]{:S(2)}) collective-permute-start(f16[24,4096]{1,0:T(8,128)(2,1)S(1)} %get-tuple-element.38), channel_id=1, source_target_pairs={{0,6},{1,7},{2,0},{3,1},{4,2},{5,3},{6,4},{7,5},{8,14},{9,15},{10,... | collective-permute-start | bytes 589832 | tf_op jit(solution)/shard_map/ppermute | solution.py:25
  178.4 18.5 %collective-permute-start.6 = (f16[24,4096]{1,0:T(8,128)(2,1)S(1)}, f16[24,4096]{1,0:T(8,128)(2,1)S(1)}, u32[]{:S(2)}, u32[]{:S(2)}) collective-permute-start(f16[24,4096]{1,0:T(8,128)(2,1)S(1)} %get-tuple-element.39), channel_id=1, source_target_pairs={{0,4},{1,5},{2,6},{3,7},{4,0},{5,1},{6,2},{7,3},{8,12},{9,13},{10,... | collective-permute-start | bytes 589832 | tf_op jit(solution)/shard_map/ppermute | solution.py:25
  178.8 18.2 %collective-permute-start.1 = (f16[24,4096]{1,0:T(8,128)(2,1)S(1)}, f16[24,4096]{1,0:T(8,128)(2,1)S(1)}, u32[]{:S(2)}, u32[]{:S(2)}) collective-permute-start(f16[24,4096]{1,0:T(8,128)(2,1)S(1)} %get-tuple-element.34), channel_id=1, source_target_pairs={{0,2},{1,3},{2,4},{3,5},{4,6},{5,7},{6,0},{7,1},{8,10},{9,11},{10,... | collective-permute-start | bytes 589832 | tf_op jit(solution)/shard_map/ppermute | solution.py:25
  179.4 18.8 %collective-permute-start.3 = (f16[24,4096]{1,0:T(8,128)(2,1)S(1)}, f16[24,4096]{1,0:T(8,128)(2,1)S(1)}, u32[]{:S(2)}, u32[]{:S(2)}) collective-permute-start(f16[24,4096]{1,0:T(8,128)(2,1)S(1)} %get-tuple-element.35), channel_id=1, source_target_pairs={{0,6},{1,7},{2,0},{3,1},{4,2},{5,3},{6,4},{7,5},{8,14},{9,15},{10,... | collective-permute-start | bytes 589832 | tf_op jit(solution)/shard_map/ppermute | solution.py:25
  184.1 24.9 %collective-permute-start.2 = (f16[24,4096]{1,0:T(8,128)(2,1)S(1)}, f16[24,4096]{1,0:T(8,128)(2,1)S(1)}, u32[]{:S(2)}, u32[]{:S(2)}) collective-permute-start(f16[24,4096]{1,0:T(8,128)(2,1)S(1)} %get-tuple-element.36), channel_id=1, source_target_pairs={{0,4},{1,5},{2,6},{3,7},{4,0},{5,1},{6,2},{7,3},{8,12},{9,13},{10,... | collective-permute-start | bytes 589832 | tf_op jit(solution)/shard_map/ppermute | solution.py:25
  209.3 16.3 %collective-permute-start.9 = (f32[24,4096]{1,0:T(8,128)S(1)}, f32[24,4096]{1,0:T(8,128)S(1)}, u32[]{:S(2)}, u32[]{:S(2)}) collective-permute-start(f32[24,4096]{1,0:T(8,128)S(1)} %get-tuple-element.32), channel_id=1, source_target_pairs={{0,1},{1,0},{2,9},{3,8},{4,17},{5,16},{6,25},{7,24},{8,3},{9,2},{1... | collective-permute-start | bytes 1179656 | tf_op jit(solution)/shard_map/ppermute | solution.py:90
  210.3 15.3 %collective-permute-start.8 = (f32[24,4096]{1,0:T(8,128)S(1)}, f32[24,4096]{1,0:T(8,128)S(1)}, u32[]{:S(2)}, u32[]{:S(2)}) collective-permute-start(f32[24,4096]{1,0:T(8,128)S(1)} %get-tuple-element.33), channel_id=1, source_target_pairs={{0,0},{1,1},{2,8},{3,9},{4,16},{5,17},{6,24},{7,25},{8,2},{9,3},{1... | collective-permute-start | bytes 1179656 | tf_op jit(solution)/shard_map/ppermute | solution.py:90
  226.8 101.5 %all-gather.13.cloned.1.call-start = ((), (), s32[]{:S(2)}) async-start(), calls=%async_computation.3 | async-start | bytes 3538944 | tf_op jit(solution)/shard_map/all_gather | solution.py:59
  265.8 62.5 %copy-start.7 = (bf16[192,4096]{1,0:T(8,128)(2,1)S(1)}, bf16[192,4096]{1,0:T(8,128)(2,1)}, u32[]{:S(2)}) copy-start(bf16[192,4096]{1,0:T(8,128)(2,1)} %all-gather.9.cloned.1.call-done) | copy-start | bytes 4718596
  387.7 5.7 %copy-start.5 = (bf16[1,192,8192]{2,1,0:T(8,128)(2,1)S(1)}, bf16[1,192,8192]{2,1,0:T(8,128)(2,1)}, u32[]{:S(2)}) copy-start(bf16[1,192,8192]{2,1,0:T(8,128)(2,1)} %all-gather.13.cloned.1.call-done) | copy-start | bytes 9437188
  390.9 20.8 %copy-start.4 = (f32[192,4096]{1,0:T(8,128)S(1)}, f32[192,4096]{1,0:T(8,128)}, u32[]{:S(2)}) copy-start(f32[192,4096]{1,0:T(8,128)} %get-tuple-element.17) | copy-start | bytes 9437188
  390.9 20.8 %collective-permute-start.14 = (f16[4,24,4096]{2,1,0:T(8,128)(2,1)S(1)}, f16[4,24,4096]{2,1,0:T(8,128)(2,1)S(1)}, u32[]{:S(2)}, u32[]{:S(2)}) collective-permute-start(f16[4,24,4096]{2,1,0:T(8,128)(2,1)S(1)} %fusion.16), channel_id=1, source_target_pairs={{0,1},{1,0},{2,3},{3,2},{4,5},{5,4},{6,7},{7,6},{8,9},{9,8},{10,11... | collective-permute-start | bytes 2359304 | tf_op jit(solution)/shard_map/ppermute | solution.py:18
  393.3 33.6 %collective-permute-start.10 = (f16[4,24,4096]{2,1,0:T(8,128)(2,1)S(1)}, f16[4,24,4096]{2,1,0:T(8,128)(2,1)S(1)}, u32[]{:S(2)}, u32[]{:S(2)}) collective-permute-start(f16[4,24,4096]{2,1,0:T(8,128)(2,1)S(1)} %fusion.15), channel_id=1, source_target_pairs={{0,1},{1,0},{2,3},{3,2},{4,5},{5,4},{6,7},{7,6},{8,9},{9,8},{10,11... | collective-permute-start | bytes 2359304 | tf_op jit(solution)/shard_map/ppermute | solution.py:18
  400.0 26.9 %copy-start.3 = (f32[192,4096]{1,0:T(8,128)S(1)}, f32[192,4096]{1,0:T(8,128)}, u32[]{:S(2)}) copy-start(f32[192,4096]{1,0:T(8,128)} %get-tuple-element.16) | copy-start | bytes 9437188
  412.1 19.1 %collective-permute-start.15 = (f16[24,4096]{1,0:T(8,128)(2,1)S(1)}, f16[24,4096]{1,0:T(8,128)(2,1)S(1)}, u32[]{:S(2)}, u32[]{:S(2)}) collective-permute-start(f16[24,4096]{1,0:T(8,128)(2,1)S(1)} %get-tuple-element.29), channel_id=1, source_target_pairs={{0,2},{1,3},{2,4},{3,5},{4,6},{5,7},{6,0},{7,1},{8,10},{9,11},{10,... | collective-permute-start | bytes 589832 | tf_op jit(solution)/shard_map/ppermute | solution.py:25
  412.7 18.4 %collective-permute-start.17 = (f16[24,4096]{1,0:T(8,128)(2,1)S(1)}, f16[24,4096]{1,0:T(8,128)(2,1)S(1)}, u32[]{:S(2)}, u32[]{:S(2)}) collective-permute-start(f16[24,4096]{1,0:T(8,128)(2,1)S(1)} %get-tuple-element.30), channel_id=1, source_target_pairs={{0,6},{1,7},{2,0},{3,1},{4,2},{5,3},{6,4},{7,5},{8,14},{9,15},{10,... | collective-permute-start | bytes 589832 | tf_op jit(solution)/shard_map/ppermute | solution.py:25
  416.0 15.2 %collective-permute-start.16 = (f16[24,4096]{1,0:T(8,128)(2,1)S(1)}, f16[24,4096]{1,0:T(8,128)(2,1)S(1)}, u32[]{:S(2)}, u32[]{:S(2)}) collective-permute-start(f16[24,4096]{1,0:T(8,128)(2,1)S(1)} %get-tuple-element.31), channel_id=1, source_target_pairs={{0,4},{1,5},{2,6},{3,7},{4,0},{5,1},{6,2},{7,3},{8,12},{9,13},{10,... | collective-permute-start | bytes 589832 | tf_op jit(solution)/shard_map/ppermute | solution.py:25
  427.3 9.7 %collective-permute-start.11 = (f16[24,4096]{1,0:T(8,128)(2,1)S(1)}, f16[24,4096]{1,0:T(8,128)(2,1)S(1)}, u32[]{:S(2)}, u32[]{:S(2)}) collective-permute-start(f16[24,4096]{1,0:T(8,128)(2,1)S(1)} %get-tuple-element.26), channel_id=1, source_target_pairs={{0,2},{1,3},{2,4},{3,5},{4,6},{5,7},{6,0},{7,1},{8,10},{9,11},{10,... | collective-permute-start | bytes 589832 | tf_op jit(solution)/shard_map/ppermute | solution.py:25
  427.9 10.0 %collective-permute-start.13 = (f16[24,4096]{1,0:T(8,128)(2,1)S(1)}, f16[24,4096]{1,0:T(8,128)(2,1)S(1)}, u32[]{:S(2)}, u32[]{:S(2)}) collective-permute-start(f16[24,4096]{1,0:T(8,128)(2,1)S(1)} %get-tuple-element.27), channel_id=1, source_target_pairs={{0,6},{1,7},{2,0},{3,1},{4,2},{5,3},{6,4},{7,5},{8,14},{9,15},{10,... | collective-permute-start | bytes 589832 | tf_op jit(solution)/shard_map/ppermute | solution.py:25
  431.2 14.7 %collective-permute-start.12 = (f16[24,4096]{1,0:T(8,128)(2,1)S(1)}, f16[24,4096]{1,0:T(8,128)(2,1)S(1)}, u32[]{:S(2)}, u32[]{:S(2)}) collective-permute-start(f16[24,4096]{1,0:T(8,128)(2,1)S(1)} %get-tuple-element.28), channel_id=1, source_target_pairs={{0,4},{1,5},{2,6},{3,7},{4,0},{5,1},{6,2},{7,3},{8,12},{9,13},{10,... | collective-permute-start | bytes 589832 | tf_op jit(solution)/shard_map/ppermute | solution.py:25
  431.2 16.2 %copy-start.1 = (bf16[96,4096]{1,0:T(8,128)(2,1)S(1)}, bf16[96,4096]{1,0:T(8,128)(2,1)}, u32[]{:S(2)}) copy-start(bf16[96,4096]{1,0:T(8,128)(2,1)} %param.6) | copy-start | bytes 2359300
Sparse Core Ops, SparseCore 0:
  10.7 22.3 all-gather.6
  35.8 60.4 all-gather.10
  227.0 38.7 all-gather.8
  267.8 60.4 all-gather.12
